TPU v7x, 128 devices: a whole 4x4x4 slice. The times are simulated.
128 devices in a mesh: ctx: 32 (over z, x_lo, y), tp: 4 (over x_hi, core).
Axes of the slice: x: 4 (x_hi: 2, x_lo: 2; x = x_hi * 2 + x_lo), y: 4, z: 4, core: 2. Of those that a mesh axis runs over, the one named last changes fastest.
Arguments:
- q_self: bfloat16 [6144, 2560], P('ctx', 'tp'), may hold values from -64 to 64
- k_self: bfloat16 [6144, 2560], P('ctx', 'tp'), may hold values from -64 to 64
- v_self: bfloat16 [6144, 2560], P('ctx', 'tp'), may hold values from -6 to 6
- grad_self: bfloat16 [6144, 2560], P('ctx', 'tp'), may hold values from -448 to 448
- q_cross: bfloat16 [6144, 2560], P('ctx', 'tp'), may hold values from -64 to 64
- grad_cross: bfloat16 [6144, 2560], P('ctx', 'tp'), may hold values from -80 to 80
- k_text: bfloat16 [512, 2560], P(None, 'tp'), may hold values from -64 to 64
- v_text: bfloat16 [512, 2560], P(None, 'tp'), may hold values from -6 to 6
- gain_q: float32 [2560], P('tp'), may hold values from 0.1 to 1.9
- gain_k: float32 [2560], P('tp'), may hold values from 0.1 to 1.9
- gain_cross_q: float32 [2560], P('tp'), may hold values from 0.1 to 1.9
- gain_text_k: float32 [2560], P('tp'), may hold values from 0.1 to 1.9
Outputs:
- grad_q_self: bfloat16 [6144, 2560], P('ctx', 'tp')
- grad_k_self: bfloat16 [6144, 2560], P('ctx', 'tp')
- grad_v_self: bfloat16 [6144, 2560], P('ctx', 'tp')
- grad_q_cross: bfloat16 [6144, 2560], P('ctx', 'tp')
- grad_k_text: bfloat16 [512, 2560], P(None, 'tp')
- grad_v_text: bfloat16 [512, 2560], P(None, 'tp')
All inputs are finite; a program needn't handle non-finite values.
Results may differ from a plain program's by a relative error of at most 0.034.
Values may be sent and summed in bfloat16 or wider, within the bound.
No kernel may reach another device: no remote copies, remote signals or barrier semaphores. Data moves between devices by JAX's collectives and lax.ppermute only.
A program may use at most 192 MiB of HBM per device.

v0:
```python
import jax
import jax.numpy as jnp
from jax import lax
from jax.sharding import PartitionSpec as P

HD = 128
epsilon = 1e-06


def squares(tensor):
    floats = tensor.astype(jnp.float32)
    return jnp.sum(floats * floats, axis=1)


def normalize(tensor, square_sum, gain, features):
    inverse = lax.rsqrt(square_sum / features + epsilon)[:, None]
    return ((tensor.astype(jnp.float32) * inverse * gain).astype(jnp.bfloat16), inverse)


def by_heads(tensor):
    return tensor.reshape(tensor.shape[0], -1, HD)


def into_blocks(tensor, span):
    return tensor.reshape(tensor.shape[0] // span, span, -1, HD)


def start_state(query_heads):
    row_count = query_heads.shape[0]
    head_count = query_heads.shape[1]
    return (
        jnp.full((head_count, row_count), -1e30, jnp.float32),
        jnp.zeros((head_count, row_count), jnp.float32),
        jnp.zeros((head_count, row_count), jnp.float32),
    )


def forward_step(running, query_heads, grad_heads, key_heads, value_heads):
    maximum, totals, weighted = running
    scores = jnp.einsum(
        "qhd,khd->hqk", query_heads, key_heads, preferred_element_type=jnp.float32
    ) * HD ** (-0.5)
    grad_prob = jnp.einsum(
        "qhd,khd->hqk", grad_heads, value_heads, preferred_element_type=jnp.float32
    )
    new_max = jnp.maximum(maximum, jnp.max(scores, axis=2))
    factor = jnp.exp(maximum - new_max)
    weights = jnp.exp(scores - new_max[:, :, None])
    totals = totals * factor + jnp.sum(weights, axis=2)
    weighted = weighted * factor + jnp.sum(weights * grad_prob, axis=2)
    return (new_max, totals, weighted)


def finish(running):
    maximum, totals, weighted = running
    return (maximum + jnp.log(totals), weighted / totals)


def backward_terms(query_heads, grad_heads, logsum, deltas, key_heads, value_heads):
    scaling = HD ** (-0.5)
    scores = (
        jnp.einsum("qhd,khd->hqk", query_heads, key_heads, preferred_element_type=jnp.float32)
        * scaling
    )
    probability = jnp.exp(scores - logsum[:, :, None])
    grad_prob = jnp.einsum(
        "qhd,khd->hqk", grad_heads, value_heads, preferred_element_type=jnp.float32
    )
    grad_score = (probability * (grad_prob - deltas[:, :, None])).astype(jnp.bfloat16)
    results = []
    results.append(
        jnp.einsum("hqk,khd->qhd", grad_score, key_heads, preferred_element_type=jnp.float32)
        * scaling
    )
    results.append(
        jnp.einsum("hqk,qhd->khd", grad_score, query_heads, preferred_element_type=jnp.float32)
        * scaling
    )
    results.append(
        jnp.einsum(
            "hqk,qhd->khd",
            probability.astype(jnp.bfloat16),
            grad_heads,
            preferred_element_type=jnp.float32,
        )
    )
    return results


def forward_pass(query_heads, grad_heads, key_blocks, value_blocks):

    def forward_advance(running, blocks):
        return (forward_step(running, query_heads, grad_heads, blocks[0], blocks[1]), None)

    return lax.scan(forward_advance, start_state(query_heads), (key_blocks, value_blocks))[0]


def query_pass(query_heads, grad_heads, logsum, deltas, key_blocks, value_blocks):

    def query_advance(grad_query, blocks):
        terms = backward_terms(query_heads, grad_heads, logsum, deltas, blocks[0], blocks[1])
        return (grad_query + terms[0], tuple(terms[1:]))

    return lax.scan(
        query_advance, jnp.zeros(query_heads.shape, jnp.float32), (key_blocks, value_blocks)
    )


def norm_terms(tensor, inverse, gain, gradient):
    unit_rows = tensor.astype(jnp.float32) * inverse
    scaled = gradient * gain
    return (unit_rows, scaled, jnp.sum(scaled * unit_rows, axis=1))


def norm_result(inverse, terms, summed, features):
    return (inverse * (terms[1] - terms[0] * (summed / features)[:, None])).astype(jnp.bfloat16)


def local(
    q_self,
    k_self,
    v_self,
    grad_self,
    q_cross,
    grad_cross,
    k_text,
    v_text,
    gain_q,
    gain_k,
    gain_cross_q,
    gain_text_k,
):
    features = q_self.shape[1] * lax.axis_size("tp")
    row_count = q_self.shape[0]
    text_rows = k_text.shape[0]
    span = 4 * row_count
    sums = lax.psum((squares(q_self), squares(k_self), squares(q_cross), squares(k_text)), "tp")
    query_norm, inverse_q = normalize(q_self, sums[0], gain_q, features)
    key_norm, inverse_k = normalize(k_self, sums[1], gain_k, features)
    cross_norm, inverse_c = normalize(q_cross, sums[2], gain_cross_q, features)
    text_norm, inverse_t = normalize(k_text, sums[3], gain_text_k, features)
    query_heads = by_heads(query_norm)
    grad_heads = by_heads(grad_self)
    key_all, value_all = (
        lax.all_gather(key_norm, "ctx", axis=0, tiled=True),
        lax.all_gather(v_self, "ctx", axis=0, tiled=True),
    )
    key_blocks = into_blocks(key_all, span)
    value_blocks = into_blocks(value_all, span)
    logsum, deltas = finish(forward_pass(query_heads, grad_heads, key_blocks, value_blocks))
    grad_query, stacked = query_pass(
        query_heads, grad_heads, logsum, deltas, key_blocks, value_blocks
    )
    grad_key, grad_value = (
        lax.psum_scatter(
            stacked[0].reshape(key_all.shape).astype(jnp.bfloat16),
            "ctx",
            scatter_dimension=0,
            tiled=True,
        ).astype(jnp.float32),
        lax.psum_scatter(
            stacked[1].reshape(key_all.shape).astype(jnp.bfloat16),
            "ctx",
            scatter_dimension=0,
            tiled=True,
        ).astype(jnp.float32),
    )
    cross_heads = by_heads(cross_norm)
    cross_grads = by_heads(grad_cross)
    text_heads = by_heads(text_norm)
    text_values = by_heads(v_text)
    cross_state = forward_step(
        start_state(cross_heads), cross_heads, cross_grads, text_heads, text_values
    )
    cross_logsum, cross_deltas = finish(cross_state)
    cross_terms = backward_terms(
        cross_heads, cross_grads, cross_logsum, cross_deltas, text_heads, text_values
    )
    text_key_grad, text_value_grad = (
        lax.psum(cross_terms[1].reshape(text_rows, -1).astype(jnp.bfloat16), "ctx").astype(
            jnp.float32
        ),
        lax.psum(cross_terms[2].reshape(text_rows, -1).astype(jnp.bfloat16), "ctx").astype(
            jnp.float32
        ),
    )
    pieces_q = norm_terms(q_self, inverse_q, gain_q, grad_query.reshape(row_count, -1))
    pieces_k = norm_terms(k_self, inverse_k, gain_k, grad_key.reshape(row_count, -1))
    pieces_c = norm_terms(q_cross, inverse_c, gain_cross_q, cross_terms[0].reshape(row_count, -1))
    pieces_t = norm_terms(k_text, inverse_t, gain_text_k, text_key_grad)
    row_sums = lax.psum((pieces_q[2], pieces_k[2], pieces_c[2], pieces_t[2]), "tp")
    return (
        norm_result(inverse_q, pieces_q, row_sums[0], features),
        norm_result(inverse_k, pieces_k, row_sums[1], features),
        grad_value.reshape(row_count, -1).astype(jnp.bfloat16),
        norm_result(inverse_c, pieces_c, row_sums[2], features),
        norm_result(inverse_t, pieces_t, row_sums[3], features),
        text_value_grad.astype(jnp.bfloat16),
    )


def solution(mesh):
    in_specs = (
        P("ctx", "tp"),
        P("ctx", "tp"),
        P("ctx", "tp"),
        P("ctx", "tp"),
        P("ctx", "tp"),
        P("ctx", "tp"),
        P(None, "tp"),
        P(None, "tp"),
        P("tp"),
        P("tp"),
        P("tp"),
        P("tp"),
    )
    out_specs = (
        P("ctx", "tp"),
        P("ctx", "tp"),
        P("ctx", "tp"),
        P("ctx", "tp"),
        P(None, "tp"),
        P(None, "tp"),
    )
    return jax.shard_map(local, mesh=mesh, in_specs=in_specs, out_specs=out_specs, check_vma=False)
```

profile of v0, /device:TPU:4, one launch (start us, length us, event | category | flops | bytes accessed | tf_op | source)
XLA Modules:
  0.0 1038.5 jit_solution(16445170293063702059)
XLA Ops:
  12.7 7.4 all-reduce.1
  24.9 2.1 fusion.29
  28.4 2.2 copy.95
  30.6 2.0 multiply_convert_fusion.1
  35.8 154.5 %all-gather.3.cloned.1.call-done = bf16[6144,640]{1,0:T(8,128)(2,1)} async-done(((bf16[192,640]{1,0:T(8,128)(2,1)}), bf16[6144,640]{1,0:T(8,128)(2,1)}) %all-gather.3.cloned.1.call-update) | async-done | bytes 7864336 | tf_op jit(solution)/shard_map/all_gather | solution.py:145
  190.3 18.1 %reshape.100 = bf16[8,768,5,128]{3,2,1,0:T(8,128)(2,1)} reshape(bf16[6144,640]{1,0:T(8,128)(2,1)} %all-gather.3.cloned.1.call-done) | data formatting | bytes 15728640 | tf_op jit(solution)/shard_map/reshape | solution.py:25
  208.4 9.9 copy.75
  218.4 140.3 %all-gather.5.cloned.1.call-done = bf16[6144,640]{1,0:T(8,128)(2,1)} async-done(((bf16[192,640]{1,0:T(8,128)(2,1)}), bf16[6144,640]{1,0:T(8,128)(2,1)}) %all-gather.5.cloned.1.call-update) | async-done | bytes 7864336 | tf_op jit(solution)/shard_map/all_gather | solution.py:146
  358.6 18.1 %reshape.101 = bf16[8,768,5,128]{3,2,1,0:T(8,128)(2,1)} reshape(bf16[6144,640]{1,0:T(8,128)(2,1)} %all-gather.5.cloned.1.call-done) | data formatting | bytes 15728640 | tf_op jit(solution)/shard_map/reshape | solution.py:25
  376.7 10.0 copy.73
  386.7 38.2 %while.30 = (s32[]{:T(128)}, f32[5,192]{1,0:T(8,128)S(1)}, f32[5,192]{1,0:T(8,128)S(1)}, f32[5,192]{1,0:T(8,128)S(1)}, bf16[8,768,5,128]{3,1,2,0:T(8,128)(2,1)},...) while((s32[]{:T(128)}, f32[5,192]{1,0:T(8,128)S(1)}, ...), condition=%wide.region_8.9_spmd.clone, body=%wide.region_4.8_spmd.clone.sunk | while | flops 384129600 | bytes 11374208 | solution.py:95
  386.7 1.8 bitcast_reduce_fusion.2
  388.6 2.1 fusion.112
  391.5 1.8 bitcast_reduce_fusion.2
  393.4 2.1 fusion.112
  396.3 1.8 bitcast_reduce_fusion.2
  398.2 2.1 fusion.112
  401.1 1.8 bitcast_reduce_fusion.2
  402.9 2.1 fusion.112
  405.9 1.8 bitcast_reduce_fusion.2
  407.7 2.1 fusion.112
  410.6 1.8 bitcast_reduce_fusion.2
  412.5 2.1 fusion.112
  415.4 1.8 bitcast_reduce_fusion.2
  417.3 2.1 fusion.112
  420.2 1.8 bitcast_reduce_fusion.2
  422.0 2.1 fusion.112
  425.0 96.3 %while.31 = (s32[]{:T(128)}, f32[192,5,128]{2,0,1:T(8,128)}, bf16[8,768,5,128]{3,1,2,0:T(8,128)(2,1)}, bf16[8,768,5,128]{3,1,2,0:T(8,128)(2,1)}, bf16[8,768,5,12...) while((s32[]{:T(128)}, f32[192,5,128]{2,0,1:T(8,128)}, ...), condition=%wide.region_10.0_spmd.clone, body=%wide.region_9.0_spmd.clone.sunk | while | flops 950476800 | bytes 28028344 | solution.py:104
  426.7 3.2 multiply_convert_fusion.3
  429.9 3.1 fusion.126
  434.8 2.1 bitcast_dynamic-update-slice_fusion.5
  438.7 3.2 multiply_convert_fusion.3
  441.8 3.2 fusion.126
  445.0 1.9 bitcast_dynamic-update-slice_fusion.4
  446.9 2.1 bitcast_dynamic-update-slice_fusion.5
  450.8 3.2 multiply_convert_fusion.3
  453.9 3.2 fusion.126
  459.0 2.1 bitcast_dynamic-update-slice_fusion.5
  462.8 3.2 multiply_convert_fusion.3
  466.0 3.2 fusion.126
  471.0 2.1 bitcast_dynamic-update-slice_fusion.5
  474.8 3.2 multiply_convert_fusion.3
  478.0 3.2 fusion.126
  481.2 1.8 bitcast_dynamic-update-slice_fusion.4
  483.0 2.1 bitcast_dynamic-update-slice_fusion.5
  486.9 3.2 multiply_convert_fusion.3
  490.0 3.2 fusion.126
  493.3 1.8 bitcast_dynamic-update-slice_fusion.4
  495.1 2.1 bitcast_dynamic-update-slice_fusion.5
  499.0 3.2 multiply_convert_fusion.3
  502.1 3.2 fusion.126
  505.3 1.8 bitcast_dynamic-update-slice_fusion.4
  507.1 2.1 bitcast_dynamic-update-slice_fusion.5
  511.0 3.2 multiply_convert_fusion.3
  514.1 3.2 fusion.126
  519.1 2.1 bitcast_dynamic-update-slice_fusion.5
  521.3 11.9 %copy.115 = bf16[8,768,5,128]{3,2,1,0:T(8,128)(2,1)} copy(bf16[8,768,5,128]{3,1,2,0:T(8,128)(2,1)} %get-tuple-element.108) | data formatting | bytes 15728640
  533.2 9.6 copy.124
  542.9 12.0 %copy.116 = bf16[8,768,5,128]{3,2,1,0:T(8,128)(2,1)} copy(bf16[8,768,5,128]{3,1,2,0:T(8,128)(2,1)} %get-tuple-element.109) | data formatting | bytes 15728640
  554.9 9.8 copy.123
  568.8 104.0 %all-reduce.5.cloned.1.call-done = (bf16[512,640]{0,1:T(8,128)(2,1)}, bf16[512,640]{1,0:T(8,128)(2,1)}) async-done(((bf16[512,640]{0,1:T(8,128)(2,1)}, bf16[512,640]{1,0:T(8,128)(2,1)}), (bf16[512,640]{0,1:T(8,128)(2,1)}, bf16[512,640]{1,0:T(8,128)(2,1)})) %all-reduce.5.cloned.1.call-update) | async-done | bytes 1310736 | tf_op jit(solution)/shard_map/psum | solution.py:180
  674.6 179.2 %reduce-scatter.7.cloned.1.call-done = bf16[192,640]{1,0:T(8,128)(2,1)} async-done(((bf16[6144,640]{1,0:T(8,128)(2,1)}), bf16[192,640]{1,0:T(8,128)(2,1)}) %reduce-scatter.7.cloned.1.call-update) | async-done | bytes 245776 | tf_op jit(solution)/shard_map/reduce_scatter | solution.py:155
  854.9 7.3 all-reduce
  867.7 163.5 %reduce-scatter.9.cloned.1.call-done = bf16[192,640]{1,0:T(8,128)(2,1)} async-done(((bf16[6144,640]{1,0:T(8,128)(2,1)}), bf16[192,640]{1,0:T(8,128)(2,1)}) %reduce-scatter.9.cloned.1.call-update) | async-done | bytes 245776
  (166 shorter events, 55.3 us)
Async XLA Ops:
  7.2 12.9 %copy-start.12 = (bf16[192,640]{1,0:T(8,128)(2,1)S(1)}, bf16[192,640]{1,0:T(8,128)(2,1)}, u32[]{:S(2)}) copy-start(bf16[192,640]{1,0:T(8,128)(2,1)} %param.17) | copy-start | bytes 737284
  7.2 12.9 %copy-start.23 = (f32[640]{0:T(1024)S(1)}, f32[640]{0:T(1024)}, u32[]{:S(2)}) copy-start(f32[640]{0:T(1024)} %param.25) | copy-start | bytes 7684
  7.2 14.6 %copy-start.18 = (bf16[192,640]{1,0:T(8,128)(2,1)S(1)}, bf16[192,640]{1,0:T(8,128)(2,1)}, u32[]{:S(2)}) copy-start(bf16[192,640]{1,0:T(8,128)(2,1)} %param.21) | copy-start | bytes 737284
  7.2 14.7 %copy-start.16 = (bf16[512,640]{1,0:T(8,128)(2,1)S(1)}, bf16[512,640]{1,0:T(8,128)(2,1)}, u32[]{:S(2)}) copy-start(bf16[512,640]{1,0:T(8,128)(2,1)} %param.23) | copy-start | bytes 1966084
  7.2 183.1 %all-gather.3.cloned.1.call-start = ((), (), s32[]{:S(2)}) async-start(), calls=%async_computation.2 | async-start | bytes 8110080 | tf_op jit(solution)/shard_map/all_gather | solution.py:145
  8.5 26.5 %copy-start.8 = (bf16[192,640]{0,1:T(8,128)(2,1)}, bf16[192,640]{0,1:T(8,128)(2,1)S(1)}, u32[]{:S(2)}) copy-start(bf16[192,640]{0,1:T(8,128)(2,1)S(1)} %copy.67) | copy-start | bytes 737284
  9.7 13.4 %copy-start.21 = (f32[640]{0:T(1024)S(1)}, f32[640]{0:T(1024)}, u32[]{:S(2)}) copy-start(f32[640]{0:T(1024)} %param.26) | copy-start | bytes 7684
  10.8 12.4 %copy-start.6 = (bf16[192,640]{0,1:T(8,128)(2,1)}, bf16[192,640]{0,1:T(8,128)(2,1)S(1)}, u32[]{:S(2)}) copy-start(bf16[192,640]{0,1:T(8,128)(2,1)S(1)} %copy.83) | copy-start | bytes 737284
  10.9 12.4 %copy-start.22 = (f32[640]{0:T(1024)S(1)}, f32[640]{0:T(1024)}, u32[]{:S(2)}) copy-start(f32[640]{0:T(1024)} %param.27) | copy-start | bytes 7684
  12.3 11.1 %copy-start.2 = (bf16[512,640]{0,1:T(8,128)(2,1)}, bf16[512,640]{0,1:T(8,128)(2,1)S(1)}, u32[]{:S(2)}) copy-start(bf16[512,640]{0,1:T(8,128)(2,1)S(1)} %copy.84) | copy-start | bytes 1966084
  20.9 337.7 %all-gather.5.cloned.1.call-start = ((), (), s32[]{:S(2)}) async-start(), calls=%async_computation.3 | async-start | bytes 8110080 | tf_op jit(solution)/shard_map/all_gather | solution.py:146
  21.7 651.1 %all-reduce.5.cloned.1.call-start = ((), (), s32[]{:S(2)}) async-start(), calls=%async_computation.6 | async-start | bytes 2621440 | tf_op jit(solution)/shard_map/psum | solution.py:180
  23.0 1.8 copy-start.14
  23.4 0.8 copy-start.10
  30.6 4.5 copy-start.20
  32.5 1.0 copy-start.4
  33.5 1.9 copy-start.19
  34.7 819.0 %reduce-scatter.7.cloned.1.call-start = ((), (), s32[]{:S(2)}) async-start(), calls=%async_computation.4 | async-start | bytes 8110080 | tf_op jit(solution)/shard_map/reduce_scatter | solution.py:155
  429.9 3.1 copy-start
  441.8 3.2 copy-start
  453.9 3.2 copy-start
  466.0 3.2 copy-start
  478.0 3.2 copy-start
  490.0 3.2 copy-start
  502.1 3.2 copy-start
  514.1 3.2 copy-start
  542.9 488.3 %reduce-scatter.9.cloned.1.call-start = ((), (), s32[]{:S(2)}) async-start(), calls=%async_computation.5 | async-start | bytes 8110080
  564.7 1.2 copy-start.5
  564.7 1.4 copy-start.11
  566.1 2.5 copy-start.7
  566.1 106.7 %copy-start.3 = (bf16[512,640]{0,1:T(8,128)(2,1)S(1)}, bf16[512,640]{0,1:T(8,128)(2,1)}, u32[]{:S(2)}) copy-start(bf16[512,640]{0,1:T(8,128)(2,1)} %copy-done.2) | copy-start | bytes 1966084
  566.1 108.1 %copy-start.1 = (f32[192,5,128]{2,0,1:T(8,128)S(1)}, f32[192,5,128]{2,0,1:T(8,128)}, u32[]{:S(2)}) copy-start(f32[192,5,128]{2,0,1:T(8,128)} %get-tuple-element.107) | copy-start | bytes 1474564
  566.1 108.3 %copy-start.9 = (bf16[192,640]{0,1:T(8,128)(2,1)S(1)}, bf16[192,640]{0,1:T(8,128)(2,1)}, u32[]{:S(2)}) copy-start(bf16[192,640]{0,1:T(8,128)(2,1)} %copy-done.8) | copy-start | bytes 737284
  567.3 286.5 %copy-start.13 = (bf16[192,640]{1,0:T(8,128)(2,1)S(1)}, bf16[192,640]{1,0:T(8,128)(2,1)}, u32[]{:S(2)}) copy-start(bf16[192,640]{1,0:T(8,128)(2,1)} %param.17) | copy-start | bytes 737284
  862.3 4.4 copy-start.15
  863.2 168.0 %copy-start.17 = (bf16[512,640]{1,0:T(8,128)(2,1)S(1)}, bf16[512,640]{1,0:T(8,128)(2,1)}, u32[]{:S(2)}) copy-start(bf16[512,640]{1,0:T(8,128)(2,1)} %get-tuple-element.486) | copy-start | bytes 1966084
Sparse Core Ops, SparseCore 0:
  21.1 169.2 all-gather.2
  192.0 166.6 all-gather.4
  361.7 310.9 all-reduce.4
  675.2 178.5 reduce-scatter.6
  856.6 174.5 reduce-scatter.8
where the time goes:
time: 1040 us
  waiting for transfers between devices  742 us (71%)
  matrix products  134 us (13%)
  local copies, waits for them, and re-layouts  116 us (11%)
  other arithmetic  16.5 us (2%)
  blocking collectives  14.6 us (1%)
  between operations  14.2 us (1%)
    reduce_scatter x1, waiting for transfers between devices, local(): lax.psum_scatter(stacked[0].reshape(key_all.shape).astype(jnp.bfloat16),...  179 us
    unnamed x6, waiting for transfers between devices  164 us
    all_gather x1, waiting for transfers between devices, local(): lax.all_gather(key_norm, 'ctx', axis=0, tiled=True)  155 us
    all_gather x1, waiting for transfers between devices, local(): lax.all_gather(v_self, 'ctx', axis=0, tiled=True)  140 us
    psum x1, waiting for transfers between devices, local(): lax.psum(cross_terms[1].reshape(text_rows, -1).astype(jnp.bfloat16), 'ctx')  104 us
    unnamed x64, local copies, waits for them, and re-layouts  75.8 us
    reshape x2, local copies, waits for them, and re-layouts, into_blocks(): return tensor.reshape(tensor.shape[0] // span, span, -1, HD)  36.2 us
    dot_general x9, matrix products, backward_terms(): jnp.einsum('qhd,khd->hqk', grad_heads, value_heads, preferred_element_typ...  27.4 us
  transfers between devices with their start and end apart: 5, of which 5 were waited for; matrix products, arithmetic and copies ran while one was open for 25% of the time, Pallas kernels for 0%

commit v1 on v0

--- a/solution.py
+++ b/solution.py
@@ -177,9 +177,10 @@
         cross_heads, cross_grads, cross_logsum, cross_deltas, text_heads, text_values
     )
     text_key_grad, text_value_grad = (
-        lax.psum(cross_terms[1].reshape(text_rows, -1).astype(jnp.bfloat16), "ctx").astype(
-            jnp.float32
-        ),
+        jnp.sum(
+            lax.all_gather(cross_terms[1].reshape(text_rows, -1).astype(jnp.bfloat16), "ctx"),
+            axis=0,
+        ).astype(jnp.float32),
         lax.psum(cross_terms[2].reshape(text_rows, -1).astype(jnp.bfloat16), "ctx").astype(
             jnp.float32
         ),

time: 1040 us -> 1450 us (1.39)
  waiting for transfers between devices: 742 us -> 1130 us
    all_gather x0 -> x1, waiting for transfers between devices: none -> 231 us  [local(): lax.all_gather(cross_terms[1].reshape(text_rows, -1).astype(jnp.bfloat16)...]
    psum x1, waiting for transfers between devices: 104 us -> 273 us  [local(): lax.psum(cross_terms[2].reshape(text_rows, -1).astype(jnp.bfloat16), 'ctx')]
    reduce_scatter x1, waiting for transfers between devices: 179 us -> 135 us  [local(): lax.psum_scatter(stacked[0].reshape(key_all.shape).astype(jnp.bfloat16),...]
    unnamed x6 -> x7, waiting for transfers between devices: 164 us -> 181 us
    unnamed x64 -> x50, local copies, waits for them, and re-layouts: 75.8 us -> 74.3 us
  transfers between devices with their start and end apart: 5 -> 6, of which waited for: 5 -> 6; matrix products, arithmetic and copies ran while one was open for 25% -> 6% of each run, Pallas kernels for 0% -> 0%
where the time goes in v1:
time: 1450 us; the launch traced here: 1440 us
  waiting for transfers between devices  1130 us (78%)
  matrix products  135 us (9%)
  local copies, waits for them, and re-layouts  118 us (8%)
  other arithmetic  30.1 us (2%)
  blocking collectives  15.3 us (1%)
  between operations  14.5 us (1%)
    psum x1, waiting for transfers between devices, local(): lax.psum(cross_terms[2].reshape(text_rows, -1).astype(jnp.bfloat16), 'ctx')  273 us
    all_gather x1, waiting for transfers between devices, local(): lax.all_gather(cross_terms[1].reshape(text_rows, -1).astype(jnp.bfloat16)...  231 us
    unnamed x7, waiting for transfers between devices  181 us
    all_gather x1, waiting for transfers between devices, local(): lax.all_gather(key_norm, 'ctx', axis=0, tiled=True)  168 us
    all_gather x1, waiting for transfers between devices, local(): lax.all_gather(v_self, 'ctx', axis=0, tiled=True)  140 us
    reduce_scatter x1, waiting for transfers between devices, local(): lax.psum_scatter(stacked[0].reshape(key_all.shape).astype(jnp.bfloat16),...  135 us
    unnamed x50, local copies, waits for them, and re-layouts  74.3 us
    reshape x2, local copies, waits for them, and re-layouts, into_blocks(): return tensor.reshape(tensor.shape[0] // span, span, -1, HD)  36.2 us
  transfers between devices with their start and end apart: 6, of which 6 were waited for; matrix products, arithmetic and copies ran while one was open for 6% of the time, Pallas kernels for 0%

profile of v1, /device:TPU:4, one launch (start us, length us, event | category | flops | bytes accessed | tf_op | source)
XLA Modules:
  0.0 1441.8 jit_solution(8070574441974994948)
XLA Ops:
  12.3 7.4 all-reduce.1
  23.2 167.7 %all-gather.4.cloned.1.call-done = bf16[6144,640]{1,0:T(8,128)(2,1)} async-done(((bf16[192,640]{1,0:T(8,128)(2,1)}), bf16[6144,640]{1,0:T(8,128)(2,1)}) %all-gather.4.cloned.1.call-update) | async-done | bytes 7864336 | tf_op jit(solution)/shard_map/all_gather | solution.py:145
  190.9 18.1 %reshape.110 = bf16[8,768,5,128]{3,2,1,0:T(8,128)(2,1)} reshape(bf16[6144,640]{1,0:T(8,128)(2,1)} %all-gather.4.cloned.1.call-done) | data formatting | bytes 15728640 | tf_op jit(solution)/shard_map/reshape | solution.py:25
  209.0 9.9 copy.108
  218.9 140.3 %all-gather.6.cloned.1.call-done = bf16[6144,640]{1,0:T(8,128)(2,1)} async-done(((bf16[192,640]{1,0:T(8,128)(2,1)}), bf16[6144,640]{1,0:T(8,128)(2,1)}) %all-gather.6.cloned.1.call-update) | async-done | bytes 7864336 | tf_op jit(solution)/shard_map/all_gather | solution.py:146
  359.2 18.1 %reshape.111 = bf16[8,768,5,128]{3,2,1,0:T(8,128)(2,1)} reshape(bf16[6144,640]{1,0:T(8,128)(2,1)} %all-gather.6.cloned.1.call-done) | data formatting | bytes 15728640 | tf_op jit(solution)/shard_map/reshape | solution.py:25
  377.3 10.0 copy.106
  387.3 38.2 %while.30 = (s32[]{:T(128)}, f32[5,192]{1,0:T(8,128)S(1)}, f32[5,192]{1,0:T(8,128)S(1)}, f32[5,192]{1,0:T(8,128)S(1)}, bf16[8,768,5,128]{3,1,2,0:T(8,128)(2,1)},...) while((s32[]{:T(128)}, f32[5,192]{1,0:T(8,128)S(1)}, ...), condition=%wide.region_8.9_spmd.clone, body=%wide.region_4.8_spmd.clone.sunk | while | flops 384129600 | bytes 11374208 | solution.py:95
  389.1 2.1 fusion.112
  392.0 1.8 bitcast_reduce_fusion.2
  393.9 2.1 fusion.112
  396.8 1.8 bitcast_reduce_fusion.2
  398.7 2.1 fusion.112
  401.6 1.8 bitcast_reduce_fusion.2
  403.5 2.1 fusion.112
  406.4 1.8 bitcast_reduce_fusion.2
  408.2 2.1 fusion.112
  411.1 1.8 bitcast_reduce_fusion.2
  413.0 2.1 fusion.112
  415.9 1.8 bitcast_reduce_fusion.2
  417.8 2.1 fusion.112
  420.7 1.8 bitcast_reduce_fusion.2
  422.6 2.1 fusion.112
  425.5 96.2 %while.31 = (s32[]{:T(128)}, f32[192,5,128]{2,0,1:T(8,128)}, bf16[8,768,5,128]{3,1,2,0:T(8,128)(2,1)}, bf16[8,768,5,128]{3,1,2,0:T(8,128)(2,1)}, bf16[8,768,5,12...) while((s32[]{:T(128)}, f32[192,5,128]{2,0,1:T(8,128)}, ...), condition=%wide.region_10.0_spmd.clone, body=%wide.region_9.0_spmd.clone.sunk | while | flops 950476800 | bytes 28028344 | solution.py:104
  427.2 3.2 multiply_convert_fusion.3
  430.4 3.1 fusion.126
  435.3 2.2 bitcast_dynamic-update-slice_fusion.5
  439.2 3.2 multiply_convert_fusion.3
  442.4 3.2 fusion.126
  445.6 1.9 bitcast_dynamic-update-slice_fusion.4
  447.4 2.1 bitcast_dynamic-update-slice_fusion.5
  451.3 3.2 multiply_convert_fusion.3
  454.4 3.2 fusion.126
  459.4 2.1 bitcast_dynamic-update-slice_fusion.5
  463.3 3.2 multiply_convert_fusion.3
  466.5 3.2 fusion.126
  471.5 2.1 bitcast_dynamic-update-slice_fusion.5
  475.3 3.2 multiply_convert_fusion.3
  478.5 3.2 fusion.126
  483.5 2.1 bitcast_dynamic-update-slice_fusion.5
  487.3 3.2 multiply_convert_fusion.3
  490.5 3.2 fusion.126
  493.7 1.8 bitcast_dynamic-update-slice_fusion.4
  495.6 2.1 bitcast_dynamic-update-slice_fusion.5
  499.4 3.2 multiply_convert_fusion.3
  502.5 3.2 fusion.126
  507.6 2.1 bitcast_dynamic-update-slice_fusion.5
  511.4 3.2 multiply_convert_fusion.3
  514.6 3.2 fusion.126
  519.6 2.1 bitcast_dynamic-update-slice_fusion.5
  521.7 11.9 copy.148
  533.6 9.6 copy.157
  552.4 2.2 copy.127
  556.1 2.2 copy.129
  558.3 12.0 copy.149
  570.3 9.8 copy.156
  581.4 2.4 fusion.41
  587.5 135.0 %reduce-scatter.7.cloned.1.call-done = bf16[192,640]{1,0:T(8,128)(2,1)} async-done(((bf16[6144,640]{1,0:T(8,128)(2,1)}), bf16[192,640]{1,0:T(8,128)(2,1)}) %reduce-scatter.7.cloned.1.call-update) | async-done | bytes 245776 | tf_op jit(solution)/shard_map/reduce_scatter | solution.py:155
  723.8 230.7 %all-gather.8.cloned.1.call-done = bf16[32,512,640]{2,1,0:T(8,128)(2,1)} async-done(((bf16[1,512,640]{2,1,0:T(8,128)(2,1)}), bf16[32,512,640]{2,1,0:T(8,128)(2,1)}) %all-gather.8.cloned.1.call-update) | async-done | bytes 20971536 | tf_op jit(solution)/shard_map/all_gather | solution.py:181
  954.5 11.0 reduce_sum.129
  965.9 7.9 all-reduce
  980.0 272.5 %all-reduce.4.cloned.1.call-done = bf16[512,640]{1,0:T(8,128)(2,1)} async-done(((bf16[512,640]{1,0:T(8,128)(2,1)}), bf16[512,640]{1,0:T(8,128)(2,1)}) %all-reduce.4.cloned.1.call-update) | async-done | bytes 655376 | tf_op jit(solution)/shard_map/psum | solution.py:184
  1252.6 180.4 %reduce-scatter.9.cloned.1.call-done = bf16[192,640]{1,0:T(8,128)(2,1)} async-done(((bf16[6144,640]{1,0:T(8,128)(2,1)}), bf16[192,640]{1,0:T(8,128)(2,1)}) %reduce-scatter.9.cloned.1.call-update) | async-done | bytes 245776
  1433.0 2.0 copy.185
  (158 shorter events, 64.5 us)
Async XLA Ops:
  7.2 15.2 %copy-start.14 = (f32[640]{0:T(1024)S(1)}, f32[640]{0:T(1024)}, u32[]{:S(2)}) copy-start(f32[640]{0:T(1024)} %param.24) | copy-start | bytes 7684
  7.2 15.6 %copy-start.12 = (bf16[192,640]{1,0:T(8,128)(2,1)S(1)}, bf16[192,640]{1,0:T(8,128)(2,1)}, u32[]{:S(2)}) copy-start(bf16[192,640]{1,0:T(8,128)(2,1)} %param.19) | copy-start | bytes 737284
  7.2 183.7 %all-gather.4.cloned.1.call-start = ((), (), s32[]{:S(2)}) async-start(), calls=%async_computation.2 | async-start | bytes 8110080 | tf_op jit(solution)/shard_map/all_gather | solution.py:145
  8.4 200.6 %copy-start.7 = (bf16[192,640]{0,1:T(8,128)(2,1)}, bf16[192,640]{0,1:T(8,128)(2,1)S(1)}, u32[]{:S(2)}) copy-start(bf16[192,640]{0,1:T(8,128)(2,1)S(1)} %copy.100) | copy-start | bytes 737284
  10.7 11.8 copy-start.5
  21.5 337.7 %all-gather.6.cloned.1.call-start = ((), (), s32[]{:S(2)}) async-start(), calls=%async_computation.3 | async-start | bytes 8110080 | tf_op jit(solution)/shard_map/all_gather | solution.py:146
  22.3 700.3 %reduce-scatter.7.cloned.1.call-start = ((), (), s32[]{:S(2)}) async-start(), calls=%async_computation.6 | async-start | bytes 8110080 | tf_op jit(solution)/shard_map/reduce_scatter | solution.py:155
  430.4 3.1 copy-start
  442.4 3.2 copy-start
  454.4 3.2 copy-start
  466.5 3.2 copy-start
  478.5 3.2 copy-start
  490.5 3.2 copy-start
  502.5 3.2 copy-start
  514.6 3.2 copy-start
  543.3 1.1 copy-start.2
  543.3 1.1 copy-start.17
  543.3 2.4 copy-start.13
  543.3 2.6 copy-start.11
  543.3 3.7 copy-start.6
  543.3 3.7 copy-start.15
  543.3 411.1 %all-gather.8.cloned.1.call-start = ((), (), s32[]{:S(2)}) async-start(), calls=%async_computation.4 | async-start | bytes 21626880 | tf_op jit(solution)/shard_map/all_gather | solution.py:181
  547.0 1.9 copy-start.10
  550.2 1.0 copy-start.3
  554.6 698.0 %all-reduce.4.cloned.1.call-start = ((), (), s32[]{:S(2)}) async-start(), calls=%async_computation.5 | async-start | bytes 1310720 | tf_op jit(solution)/shard_map/psum | solution.py:184
  558.3 874.7 %reduce-scatter.9.cloned.1.call-start = ((), (), s32[]{:S(2)}) async-start(), calls=%async_computation.7 | async-start | bytes 8110080
  580.2 1.2 copy-start.4
  581.4 3.8 copy-start.1
  581.4 4.9 copy-start.8
  581.4 141.2 %copy-start.9 = (bf16[192,640]{1,0:T(8,128)(2,1)S(1)}, bf16[192,640]{1,0:T(8,128)(2,1)}, u32[]{:S(2)}) copy-start(bf16[192,640]{1,0:T(8,128)(2,1)} %param.17) | copy-start | bytes 737284
  581.4 141.2 %copy-start.16 = (f32[640]{0:T(1024)S(1)}, f32[640]{0:T(1024)}, u32[]{:S(2)}) copy-start(f32[640]{0:T(1024)} %param.25) | copy-start | bytes 7684
Sparse Core Ops, SparseCore 0:
  21.6 169.2 all-gather.3
  192.6 166.6 all-gather.5
  543.4 179.1 reduce-scatter.6
  724.2 230.2 all-gather.7
  957.0 295.5 all-reduce.3
  1255.4 177.4 reduce-scatter.8
